TPU v7x, 256 devices: a whole 4x4x8 slice. The times are simulated.
256 devices in a mesh: slab: 32 (over z_lo, y, core), tm: 8 (over x, z_hi).
Axes of the slice: x: 4, y: 4, z: 8 (z_hi: 2, z_lo: 4; z = z_hi * 4 + z_lo), core: 2. Of those that a mesh axis runs over, the one named last changes fastest.
Arguments:
- recording: bfloat16 [512, 65536], P('tm', 'slab'), may hold values from -6 to 6
- footprints: bfloat16 [2176, 8192], P(None, 'slab'), may hold values from -0.125 to 0.125
- traces: float32 [512, 8192], P('tm', 'slab'), may hold values from 0 to 2
- live_count: int32 [32], replicated, may hold values from 1 to 256, 6144 in all
Outputs:
- new_traces: float32 [512, 8192], P('tm', 'slab')
- new_footprints: bfloat16 [2176, 8192], P('tm', 'slab')
Inputs may be any that keep to these rules, and one draw needn't show every extreme that they name: Slots 0 .. live_count[s] - 1 of slab s are live; some slab has all 256 live.
All inputs are finite; a program needn't handle non-finite values.
Results may differ from a plain program's by a relative error of at most 0.0034.
Values may be sent and summed in bfloat16 or wider, within the bound.
A program may use at most 64 MiB of HBM per device.

v0:
```python
import jax
import jax.numpy as jnp
from jax import lax
from jax.sharding import PartitionSpec as P

GROUP = 128
GROUPS_DEV = 2


def passed_along(block, axis, distance):
    devices = range(lax.axis_size(axis))
    route = [(i - distance, i) for i in devices if i - distance in devices]
    return lax.ppermute(block, axis, route)


def with_halo(cells, sides, width):
    for axis, dim in sides:
        count = lax.axis_size(axis)
        ends = count - 1
        head = lax.slice_in_dim(cells, 0, width, axis=dim)
        tail = lax.slice_in_dim(cells, cells.shape[dim] - width, cells.shape[dim], axis=dim)
        cells = jnp.concatenate(
            [
                lax.ppermute(tail, axis, [(i, (i + 1) % count) for i in range(ends)]),
                cells,
                lax.ppermute(head, axis, [((i + 1) % count, i) for i in range(ends)]),
            ],
            axis=dim,
        )
    return cells


def contract_first(left, right):
    return lax.dot_general(
        left, right, (((0,), (0,)), ((), ())), preferred_element_type=jnp.float32
    )


def on_device(recording, footprints, traces, live_count):
    slabs = lax.axis_size("slab")
    slab_index = lax.axis_index("slab")
    neurons = traces.shape[1]
    extended = footprints.shape[0]
    voxels = recording.shape[1]
    rim_rows = extended - voxels
    slots = jnp.arange(neurons, dtype=jnp.int32)
    live_here = jnp.sum(jnp.where(jnp.arange(slabs, dtype=jnp.int32) == slab_index, live_count, 0))
    living = slots < live_here
    row_ids = jnp.arange(extended, dtype=jnp.int32)
    kept_mask = living[None, :] & ((row_ids[:, None] < voxels) | (slab_index < slabs - 1))
    masked_foot = jnp.where(kept_mask, footprints, jnp.zeros_like(footprints))
    start_tr = jnp.where(living[None, :], traces, jnp.zeros_like(traces))
    next_edge, movie_rim = passed_along(
        (masked_foot[:rim_rows], recording[:, :rim_rows]), "slab", -1
    )
    prev_rim = passed_along(masked_foot[voxels:], "slab", 1)
    movie_ext = jnp.concatenate([recording, movie_rim], 1)
    drive = jnp.dot(movie_ext, masked_foot, preferred_element_type=jnp.float32)
    gram_own = contract_first(masked_foot, masked_foot)
    gram_prev = contract_first(masked_foot[:rim_rows], prev_rim)
    gram_next = contract_first(masked_foot[voxels:], next_edge)
    diag_own = jnp.diagonal(gram_own) + 1e-06
    halo_tr = with_halo(start_tr, (("slab", 1),), neurons)
    prev_c = halo_tr[:, :neurons]
    next_c = halo_tr[:, 2 * neurons :]
    outside = jnp.dot(prev_c, gram_prev.T, precision=lax.Precision.HIGHEST) + jnp.dot(
        next_c, gram_next.T, precision=lax.Precision.HIGHEST
    )

    def sweep(group_id, current):
        offset = group_id * GROUP
        columns = lax.dynamic_slice_in_dim(gram_own, offset, GROUP, 1)
        coupled = jnp.dot(
            current, columns, precision=lax.Precision.HIGHEST
        ) + lax.dynamic_slice_in_dim(outside, offset, GROUP, 1)
        before = lax.dynamic_slice_in_dim(current, offset, GROUP, 1)
        driven = lax.dynamic_slice_in_dim(drive, offset, GROUP, 1)
        scaled = lax.dynamic_slice_in_dim(diag_own, offset, GROUP, 0)
        updated = jnp.maximum(before + (driven - coupled) / scaled, 0.0)
        return lax.dynamic_update_slice_in_dim(current, updated, offset, 1)

    new_tr = lax.fori_loop(0, GROUPS_DEV, sweep, start_tr)
    rounded = new_tr.astype(jnp.bfloat16)
    side_tr = with_halo(rounded, (("slab", 1),), neurons)
    frames_all = lax.all_gather(side_tr, "tm", axis=0, tiled=True)
    prev_all = frames_all[:, :neurons]
    own_all = frames_all[:, neurons : 2 * neurons]
    next_all = frames_all[:, 2 * neurons :]
    q_own = contract_first(own_all, own_all)
    q_prev = contract_first(prev_all, own_all)
    q_next = contract_first(next_all, own_all)
    divisor = jnp.maximum(jnp.diagonal(q_own), 1.0)
    share_rows = extended // lax.axis_size("tm")
    first_row = lax.axis_index("tm") * share_rows
    blocks = lax.all_to_all(movie_ext, "tm", split_axis=1, concat_axis=0, tiled=True)
    proj_rows = contract_first(blocks, own_all)
    zero_rows = jnp.zeros((voxels, neurons), jnp.bfloat16)
    prev_full = jnp.concatenate([prev_rim, zero_rows], 0)
    next_full = jnp.concatenate([zero_rows, next_edge], 0)
    foot_share = lax.dynamic_slice_in_dim(masked_foot, first_row, share_rows, 0).astype(jnp.float32)
    prev_share = lax.dynamic_slice_in_dim(prev_full, first_row, share_rows, 0).astype(jnp.float32)
    next_share = lax.dynamic_slice_in_dim(next_full, first_row, share_rows, 0).astype(jnp.float32)
    coupling = jnp.dot(foot_share, q_own, precision=lax.Precision.HIGHEST)
    coupling = coupling + jnp.dot(prev_share, q_prev, precision=lax.Precision.HIGHEST)
    coupling = coupling + jnp.dot(next_share, q_next, precision=lax.Precision.HIGHEST)
    new_foot = jnp.maximum(foot_share + (proj_rows - coupling) / divisor, 0.0).astype(jnp.bfloat16)
    return (new_tr, new_foot)


def solution(mesh):
    placed = (P("tm", "slab"), P(None, "slab"), P("tm", "slab"), P())
    return jax.shard_map(
        on_device,
        mesh=mesh,
        in_specs=placed,
        out_specs=(P("tm", "slab"), P("tm", "slab")),
        check_vma=False,
    )
```

profile of v0, /device:TPU:32, one launch (start us, length us, event | category | flops | bytes accessed | tf_op | source)
XLA Modules:
  0.0 112.4 jit_solution(6685149426623411708)
XLA Ops:
  0.6 1.3 %fusion.26 = s32[]{:T(128)} fusion(s32[32]{0:T(128)} %param.9, s32[]{:T(128)S(6)} %axis_index.23), kind=kLoop, calls=%fused_computation.45 | loop fusion | flops 95 | bytes 136 | tf_op jit(solution)/shard_map/reduce_sum | solution.py:47
  1.9 0.6 iota_compare_fusion.1
  2.6 0.8 broadcast_select_fusion
  3.4 3.9 %collective-permute-start.3 = (f32[64,256]{1,0:T(8,128)S(1)}, f32[64,256]{1,0:T(8,128)S(1)}, u32[]{:S(2)}, u32[]{:S(2)}) collective-permute-start(f32[64,256]{1,0:T(8,128)S(1)} %broadcast_select_fusion), channel_id=1, source_target_pairs={{8,0},{16,8},{24,16},{32,24},{40,32},{48,40},{56,48},{64,56},{72,6... | collective-permute-start | bytes 196616 | tf_op jit(solution)/shard_map/ppermute | solution.py:26
  7.3 1.9 %collective-permute-start.1 = (f32[64,256]{1,0:T(8,128)S(1)}, f32[64,256]{1,0:T(8,128)S(1)}, u32[]{:S(2)}, u32[]{:S(2)}) collective-permute-start(f32[64,256]{1,0:T(8,128)S(1)} %broadcast_select_fusion), channel_id=1, source_target_pairs={{0,8},{8,16},{16,24},{24,32},{32,40},{40,48},{48,56},{56,64},{64,7... | collective-permute-start | bytes 196616 | tf_op jit(solution)/shard_map/ppermute | solution.py:24
  9.3 0.0 copy-start.1
  9.3 2.3 %and_select_fusion = bf16[2176,256]{1,0:T(8,128)(2,1)S(1)} fusion(bf16[2176,256]{1,0:T(8,128)(2,1)} %param.7, pred[256]{0:T(512)(128)(4,1)S(1)} %iota_compare_fusion.1, pred[2176]{0:T(1024)(128)(4,1)S(1)} %fusion.22), kind=kLoop, calls=%fused_computation.11 | loop fusion | flops 1114112 | bytes 2230656 | tf_op jit(solution)/shard_map/jit(_where)/select_n | solution.py:51
  11.6 5.8 %collective-permute-start.4 = (bf16[128,256]{1,0:T(8,128)(2,1)S(1)}, bf16[128,256]{1,0:T(8,128)(2,1)S(1)}, u32[]{:S(2)}, u32[]{:S(2)}) collective-permute-start(bf16[128,256]{1,0:T(8,128)(2,1)S(1)} %get-tuple-element.125), channel_id=1, source_target_pairs={{8,0},{16,8},{24,16},{32,24},{40,32},{48,40},{56,48},{64,56},{72,6... | collective-permute-start | bytes 196616 | tf_op jit(solution)/shard_map/ppermute | solution.py:13
  17.3 1.9 %collective-permute-start.2 = (bf16[128,256]{1,0:T(8,128)(2,1)S(1)}, bf16[128,256]{1,0:T(8,128)(2,1)S(1)}, u32[]{:S(2)}, u32[]{:S(2)}) collective-permute-start(bf16[128,256]{1,0:T(8,128)(2,1)S(1)} %get-tuple-element.124), channel_id=1, source_target_pairs={{0,8},{8,16},{16,24},{24,32},{32,40},{40,48},{48,56},{56,64},{64,7... | collective-permute-start | bytes 196616 | tf_op jit(solution)/shard_map/ppermute | solution.py:13
  19.3 0.0 copy-done.1
  19.3 5.8 %collective-permute-start = (bf16[64,128]{1,0:T(8,128)(2,1)S(1)}, bf16[64,128]{1,0:T(8,128)(2,1)S(1)}, u32[]{:S(2)}, u32[]{:S(2)}) collective-permute-start(bf16[64,128]{1,0:T(8,128)(2,1)S(1)} %slice.20), channel_id=1, source_target_pairs={{8,0},{16,8},{24,16},{32,24},{40,32},{48,40},{56,48},{64,56},{72,6... | collective-permute-start | bytes 49160 | tf_op jit(solution)/shard_map/ppermute | solution.py:13
  25.1 0.5 fusion.35
  25.6 2.3 %gather_fusion = f32[256]{0:T(256)S(1)} fusion(f32[256,256]{1,0:T(8,128)S(1)} %fusion.35, s32[256]{0:T(256)S(1)} %bitcast.35), kind=kCustom, calls=%fused_computation | custom fusion | bytes 4096 | tf_op jit(solution)/shard_map/jit(diagonal)/cond/branch_0_fun/gather | solution.py:62
  28.0 0.0 collective-permute-done
  28.0 0.3 fusion.34
  28.3 0.0 collective-permute-done.4
  28.3 0.2 fusion.29
  28.5 0.0 collective-permute-done.2
  28.5 0.2 fusion.31
  28.8 0.0 collective-permute-done.3
  28.8 0.4 fusion.36
  29.1 0.0 collective-permute-done.1
  29.1 0.4 convolution_add_fusion.2
  29.5 0.7 while.13
  29.5 0.1 dynamic_slice.68
  29.6 0.2 fusion.57
  29.9 0.1 dynamic_slice.68
  29.9 0.2 fusion.57
  30.2 0.0 copy-start
  30.2 1.9 %collective-permute-start.5 = (bf16[64,256]{1,0:T(8,128)(2,1)S(1)}, bf16[64,256]{1,0:T(8,128)(2,1)S(1)}, u32[]{:S(2)}, u32[]{:S(2)}) collective-permute-start(bf16[64,256]{1,0:T(8,128)(2,1)S(1)} %convert_element_type.12), channel_id=1, source_target_pairs={{0,8},{8,16},{16,24},{24,32},{32,40},{40,48},{48,56},{56,64},{64,7... | collective-permute-start | bytes 98312 | tf_op jit(solution)/shard_map/ppermute | solution.py:24
  32.2 5.8 %collective-permute-start.6 = (bf16[64,256]{1,0:T(8,128)(2,1)S(1)}, bf16[64,256]{1,0:T(8,128)(2,1)S(1)}, u32[]{:S(2)}, u32[]{:S(2)}) collective-permute-start(bf16[64,256]{1,0:T(8,128)(2,1)S(1)} %convert_element_type.12), channel_id=1, source_target_pairs={{8,0},{16,8},{24,16},{32,24},{40,32},{48,40},{56,48},{64,56},{72,6... | collective-permute-start | bytes 98312 | tf_op jit(solution)/shard_map/ppermute | solution.py:26
  37.9 0.5 all_to_all.14
  38.4 0.8 copy.6
  39.2 0.0 copy-done
  39.2 10.9 %all-to-all-start = ((bf16[64,8,272]{2,0,1:T(8,128)(2,1)}), bf16[64,8,272]{2,0,1:T(8,128)(2,1)S(1)}, u32[]{:S(2)}, u32[]{:S(2)}) async-start(bf16[64,8,272]{2,0,1:T(8,128)(2,1)} %copy.6), calls=%async_computation | async-start | bytes 786432 | tf_op jit(solution)/shard_map/all_to_all | solution.py:95
  50.1 0.0 collective-permute-done.5
  50.1 0.0 collective-permute-done.6
  50.2 57.1 %all_gather.3 = bf16[512,768]{1,0:T(8,128)(2,1)S(1)} all-gather(bf16[64,768]{1,0:T(8,128)(2,1)S(1)} %pad_maximum_fusion), channel_id=1, replica_groups=mesh['slab'=32,'tm'=8] {'tm'}, dimensions={0}, use_global_device_ids=true | all-gather | bytes 884736 | tf_op jit(solution)/shard_map/all_gather | solution.py:85
  107.3 0.3 fusion.17
  107.5 0.3 fusion.13
  107.8 2.3 %gather_fusion.1 = f32[256]{0:T(256)S(1)} fusion(f32[256,256]{1,0:T(8,128)S(1)} %fusion.17, s32[256]{0:T(256)S(1)} %bitcast.36), kind=kCustom, calls=%fused_computation.1 | custom fusion | bytes 4096 | tf_op jit(solution)/shard_map/jit(diagonal)/cond/branch_0_fun/gather | solution.py:92
  110.1 0.3 fusion.20
  110.5 0.3 convolution_add_fusion.1
  110.8 0.3 fusion.11
  111.1 0.4 convolution_add_fusion
  111.4 0.0 all-to-all-done
  111.4 0.9 fusion.10
  (12 shorter events, 0.1 us)
Async XLA Ops:
  3.4 25.3 %collective-permute-start.3 = (f32[64,256]{1,0:T(8,128)S(1)}, f32[64,256]{1,0:T(8,128)S(1)}, u32[]{:S(2)}, u32[]{:S(2)}) collective-permute-start(f32[64,256]{1,0:T(8,128)S(1)} %broadcast_select_fusion), channel_id=1, source_target_pairs={{8,0},{16,8},{24,16},{32,24},{40,32},{48,40},{56,48},{64,56},{72,6... | collective-permute-start | bytes 196616 | tf_op jit(solution)/shard_map/ppermute | solution.py:26
  7.3 21.8 %collective-permute-start.1 = (f32[64,256]{1,0:T(8,128)S(1)}, f32[64,256]{1,0:T(8,128)S(1)}, u32[]{:S(2)}, u32[]{:S(2)}) collective-permute-start(f32[64,256]{1,0:T(8,128)S(1)} %broadcast_select_fusion), channel_id=1, source_target_pairs={{0,8},{8,16},{16,24},{24,32},{32,40},{40,48},{48,56},{56,64},{64,7... | collective-permute-start | bytes 196616 | tf_op jit(solution)/shard_map/ppermute | solution.py:24
  9.3 10.0 %copy-start.1 = (bf16[64,2048]{1,0:T(8,128)(2,1)S(1)}, bf16[64,2048]{1,0:T(8,128)(2,1)}, u32[]{:S(2)}) copy-start(bf16[64,2048]{1,0:T(8,128)(2,1)} %param.6) | copy-start | bytes 786436
  11.6 16.7 %collective-permute-start.4 = (bf16[128,256]{1,0:T(8,128)(2,1)S(1)}, bf16[128,256]{1,0:T(8,128)(2,1)S(1)}, u32[]{:S(2)}, u32[]{:S(2)}) collective-permute-start(bf16[128,256]{1,0:T(8,128)(2,1)S(1)} %get-tuple-element.125), channel_id=1, source_target_pairs={{8,0},{16,8},{24,16},{32,24},{40,32},{48,40},{56,48},{64,56},{72,6... | collective-permute-start | bytes 196616 | tf_op jit(solution)/shard_map/ppermute | solution.py:13
  17.3 11.2 %collective-permute-start.2 = (bf16[128,256]{1,0:T(8,128)(2,1)S(1)}, bf16[128,256]{1,0:T(8,128)(2,1)S(1)}, u32[]{:S(2)}, u32[]{:S(2)}) collective-permute-start(bf16[128,256]{1,0:T(8,128)(2,1)S(1)} %get-tuple-element.124), channel_id=1, source_target_pairs={{0,8},{8,16},{16,24},{24,32},{32,40},{40,48},{48,56},{56,64},{64,7... | collective-permute-start | bytes 196616 | tf_op jit(solution)/shard_map/ppermute | solution.py:13
  19.3 8.7 %collective-permute-start = (bf16[64,128]{1,0:T(8,128)(2,1)S(1)}, bf16[64,128]{1,0:T(8,128)(2,1)S(1)}, u32[]{:S(2)}, u32[]{:S(2)}) collective-permute-start(bf16[64,128]{1,0:T(8,128)(2,1)S(1)} %slice.20), channel_id=1, source_target_pairs={{8,0},{16,8},{24,16},{32,24},{40,32},{48,40},{56,48},{64,56},{72,6... | collective-permute-start | bytes 49160 | tf_op jit(solution)/shard_map/ppermute | solution.py:13
  30.2 9.0 %copy-start = (f32[64,256]{1,0:T(8,128)}, f32[64,256]{1,0:T(8,128)S(1)}, u32[]{:S(2)}) copy-start(f32[64,256]{1,0:T(8,128)S(1)} %get-tuple-element.109) | copy-start | bytes 196612
  30.2 19.9 %collective-permute-start.5 = (bf16[64,256]{1,0:T(8,128)(2,1)S(1)}, bf16[64,256]{1,0:T(8,128)(2,1)S(1)}, u32[]{:S(2)}, u32[]{:S(2)}) collective-permute-start(bf16[64,256]{1,0:T(8,128)(2,1)S(1)} %convert_element_type.12), channel_id=1, source_target_pairs={{0,8},{8,16},{16,24},{24,32},{32,40},{40,48},{48,56},{56,64},{64,7... | collective-permute-start | bytes 98312 | tf_op jit(solution)/shard_map/ppermute | solution.py:24
  32.2 18.0 %collective-permute-start.6 = (bf16[64,256]{1,0:T(8,128)(2,1)S(1)}, bf16[64,256]{1,0:T(8,128)(2,1)S(1)}, u32[]{:S(2)}, u32[]{:S(2)}) collective-permute-start(bf16[64,256]{1,0:T(8,128)(2,1)S(1)} %convert_element_type.12), channel_id=1, source_target_pairs={{8,0},{16,8},{24,16},{32,24},{40,32},{48,40},{56,48},{64,56},{72,6... | collective-permute-start | bytes 98312 | tf_op jit(solution)/shard_map/ppermute | solution.py:26
  39.2 72.2 %all-to-all-start = ((bf16[64,8,272]{2,0,1:T(8,128)(2,1)}), bf16[64,8,272]{2,0,1:T(8,128)(2,1)S(1)}, u32[]{:S(2)}, u32[]{:S(2)}) async-start(bf16[64,8,272]{2,0,1:T(8,128)(2,1)} %copy.6), calls=%async_computation | async-start | bytes 786432 | tf_op jit(solution)/shard_map/all_to_all | solution.py:95
where the time goes:
time: 113 us; the launch traced here: 112 us
  blocking collectives  57.1 us (51%)
  starting transfers between devices  37.8 us (33%)
  local copies, waits for them, and re-layouts  6.19 us (5%)
  matrix products  5.12 us (5%)
  other arithmetic  5.09 us (5%)
    all_gather x1, blocking collectives, on_device(): frames_all = lax.all_gather(side_tr, 'tm', axis=0, tiled=True)  57.1 us
    ppermute x3, starting transfers between devices, passed_along(): return lax.ppermute(block, axis, route)  13.4 us
    all_to_all x1, starting transfers between devices, on_device(): lax.all_to_all(movie_ext, 'tm', split_axis=1, concat_axis=0, tiled=True)  10.9 us
    ppermute x2, starting transfers between devices, with_halo(): lax.ppermute(head, axis, [((i + 1) % count, i) for i in range(ends)])  9.65 us
    ppermute x2, starting transfers between devices, with_halo(): lax.ppermute(tail, axis, [(i, (i + 1) % count) for i in range(ends)])  3.84 us
    dot_general x7, matrix products, contract_first(): lax.dot_general(left, right, (((0,), (0,)), ((), ())), preferred_element_...  2.64 us
    gather x1, local copies, waits for them, and re-layouts, on_device(): diag_own = jnp.diagonal(gram_own) + 1e-06  2.34 us
    gather x1, local copies, waits for them, and re-layouts, on_device(): divisor = jnp.maximum(jnp.diagonal(q_own), 1.0)  2.34 us
  transfers between devices with their start and end apart: 8, of which 0 were waited for; matrix products, arithmetic and copies ran while one was open for 10% of the time, Pallas kernels for 0%

commit v1 on v0

--- a/solution.py
+++ b/solution.py
@@ -82,7 +82,9 @@
     new_tr = lax.fori_loop(0, GROUPS_DEV, sweep, start_tr)
     rounded = new_tr.astype(jnp.bfloat16)
     side_tr = with_halo(rounded, (("slab", 1),), neurons)
-    frames_all = lax.all_gather(side_tr, "tm", axis=0, tiled=True)
+    frames_all = jnp.concatenate(
+        lax.all_to_all(jnp.stack([side_tr] * lax.axis_size("tm")), "tm", 0, 0), axis=0
+    )
     prev_all = frames_all[:, :neurons]
     own_all = frames_all[:, neurons : 2 * neurons]
     next_all = frames_all[:, 2 * neurons :]

time: 113 us -> 97.5 us (0.86)
  blocking collectives: 57.1 us -> 0 us
  waiting for transfers between devices: 0.03 us -> 37.2 us
  starting transfers between devices: 37.8 us -> 39.9 us
  local copies, waits for them, and re-layouts: 6.19 us -> 7.86 us
    all_gather x1 -> x0, blocking collectives: 57.1 us -> none  [on_device(): frames_all = lax.all_gather(side_tr, 'tm', axis=0, tiled=True)]
    all_to_all x0 -> x1, waiting for transfers between devices: none -> 20 us  [on_device(): lax.all_to_all(jnp.stack([side_tr] * lax.axis_size('tm')), 'tm', 0, 0)]
    all_to_all x1, waiting for transfers between devices: 0.01 us -> 11.8 us  [on_device(): lax.all_to_all(movie_ext, 'tm', split_axis=1, concat_axis=0, tiled=True)]
    all_to_all x0 -> x1, starting transfers between devices: none -> 10.9 us  [on_device(): lax.all_to_all(jnp.stack([side_tr] * lax.axis_size('tm')), 'tm', 0, 0)]
    all_to_all x1, starting transfers between devices: 10.9 us -> 3.45 us  [on_device(): lax.all_to_all(movie_ext, 'tm', split_axis=1, concat_axis=0, tiled=True)]
    ppermute x2, waiting for transfers between devices: 0.01 us -> 5.41 us  [with_halo(): lax.ppermute(tail, axis, [(i, (i + 1) % count) for i in range(ends)])]
    ppermute x2, starting transfers between devices: 9.65 us -> 8.3 us  [with_halo(): lax.ppermute(head, axis, [((i + 1) % count, i) for i in range(ends)])]
  transfers between devices with their start and end apart: 8 -> 9, of which waited for: 0 -> 3; matrix products, arithmetic and copies ran while one was open for 10% -> 10% of each run, Pallas kernels for 0% -> 0%
where the time goes in v1:
time: 97.5 us; the launch traced here: 96.9 us
  starting transfers between devices  39.9 us (41%)
  waiting for transfers between devices  37.2 us (38%)
  local copies, waits for them, and re-layouts  7.86 us (8%)
  matrix products  5.85 us (6%)
  other arithmetic  5.09 us (5%)
    all_to_all x1, waiting for transfers between devices, on_device(): lax.all_to_all(jnp.stack([side_tr] * lax.axis_size('tm')), 'tm', 0, 0)  20 us
    ppermute x3, starting transfers between devices, passed_along(): return lax.ppermute(block, axis, route)  13.4 us
    all_to_all x1, waiting for transfers between devices, on_device(): lax.all_to_all(movie_ext, 'tm', split_axis=1, concat_axis=0, tiled=True)  11.8 us
    all_to_all x1, starting transfers between devices, on_device(): lax.all_to_all(jnp.stack([side_tr] * lax.axis_size('tm')), 'tm', 0, 0)  10.9 us
    ppermute x2, starting transfers between devices, with_halo(): lax.ppermute(head, axis, [((i + 1) % count, i) for i in range(ends)])  8.3 us
    ppermute x2, waiting for transfers between devices, with_halo(): lax.ppermute(tail, axis, [(i, (i + 1) % count) for i in range(ends)])  5.41 us
    ppermute x2, starting transfers between devices, with_halo(): lax.ppermute(tail, axis, [(i, (i + 1) % count) for i in range(ends)])  3.84 us
    all_to_all x1, starting transfers between devices, on_device(): lax.all_to_all(movie_ext, 'tm', split_axis=1, concat_axis=0, tiled=True)  3.45 us
  transfers between devices with their start and end apart: 9, of which 3 were waited for; matrix products, arithmetic and copies ran while one was open for 10% of the time, Pallas kernels for 0%

profile of v1, /device:TPU:32, one launch (start us, length us, event | category | flops | bytes accessed | tf_op | source)
XLA Modules:
  0.0 96.9 jit_solution(12130789898216621821)
XLA Ops:
  0.6 1.3 %fusion.28 = s32[]{:T(128)} fusion(s32[32]{0:T(128)} %param.9, s32[]{:T(128)S(6)} %axis_index.23), kind=kLoop, calls=%fused_computation.46 | loop fusion | flops 95 | bytes 136 | tf_op jit(solution)/shard_map/reduce_sum | solution.py:47
  1.9 0.6 iota_compare_fusion.1
  2.6 0.8 broadcast_select_fusion
  3.4 3.9 %collective-permute-start.3 = (f32[64,256]{1,0:T(8,128)S(1)}, f32[64,256]{1,0:T(8,128)S(1)}, u32[]{:S(2)}, u32[]{:S(2)}) collective-permute-start(f32[64,256]{1,0:T(8,128)S(1)} %broadcast_select_fusion), channel_id=1, source_target_pairs={{8,0},{16,8},{24,16},{32,24},{40,32},{48,40},{56,48},{64,56},{72,6... | collective-permute-start | bytes 196616 | tf_op jit(solution)/shard_map/ppermute | solution.py:26
  7.3 1.9 %collective-permute-start.1 = (f32[64,256]{1,0:T(8,128)S(1)}, f32[64,256]{1,0:T(8,128)S(1)}, u32[]{:S(2)}, u32[]{:S(2)}) collective-permute-start(f32[64,256]{1,0:T(8,128)S(1)} %broadcast_select_fusion), channel_id=1, source_target_pairs={{0,8},{8,16},{16,24},{24,32},{32,40},{40,48},{48,56},{56,64},{64,7... | collective-permute-start | bytes 196616 | tf_op jit(solution)/shard_map/ppermute | solution.py:24
  9.3 0.7 slice.20
  10.0 5.7 %collective-permute-start = (bf16[64,128]{1,0:T(8,128)(2,1)S(1)}, bf16[64,128]{1,0:T(8,128)(2,1)S(1)}, u32[]{:S(2)}, u32[]{:S(2)}) collective-permute-start(bf16[64,128]{1,0:T(8,128)(2,1)S(1)} %slice.20), channel_id=1, source_target_pairs={{8,0},{16,8},{24,16},{32,24},{40,32},{48,40},{56,48},{64,56},{72,6... | collective-permute-start | bytes 49160 | tf_op jit(solution)/shard_map/ppermute | solution.py:13
  15.8 0.0 copy-start.1
  15.8 2.3 %and_select_fusion = bf16[2176,256]{1,0:T(8,128)(2,1)S(1)} fusion(bf16[2176,256]{1,0:T(8,128)(2,1)} %param.7, pred[256]{0:T(512)(128)(4,1)S(1)} %iota_compare_fusion.1, pred[2176]{0:T(1024)(128)(4,1)S(1)} %fusion.24), kind=kLoop, calls=%fused_computation.11 | loop fusion | flops 1114112 | bytes 2230656 | tf_op jit(solution)/shard_map/jit(_where)/select_n | solution.py:51
  18.1 1.9 %collective-permute-start.2 = (bf16[128,256]{1,0:T(8,128)(2,1)S(1)}, bf16[128,256]{1,0:T(8,128)(2,1)S(1)}, u32[]{:S(2)}, u32[]{:S(2)}) collective-permute-start(bf16[128,256]{1,0:T(8,128)(2,1)S(1)} %get-tuple-element.124), channel_id=1, source_target_pairs={{0,8},{8,16},{16,24},{24,32},{32,40},{40,48},{48,56},{56,64},{64,7... | collective-permute-start | bytes 196616 | tf_op jit(solution)/shard_map/ppermute | solution.py:13
  20.0 5.8 %collective-permute-start.4 = (bf16[128,256]{1,0:T(8,128)(2,1)S(1)}, bf16[128,256]{1,0:T(8,128)(2,1)S(1)}, u32[]{:S(2)}, u32[]{:S(2)}) collective-permute-start(bf16[128,256]{1,0:T(8,128)(2,1)S(1)} %get-tuple-element.125), channel_id=1, source_target_pairs={{8,0},{16,8},{24,16},{32,24},{40,32},{48,40},{56,48},{64,56},{72,6... | collective-permute-start | bytes 196616 | tf_op jit(solution)/shard_map/ppermute | solution.py:13
  25.8 0.0 copy-done.1
  25.8 0.5 fusion.37
  26.3 2.3 %gather_fusion = f32[256]{0:T(256)S(1)} fusion(f32[256,256]{1,0:T(8,128)S(1)} %fusion.37, s32[256]{0:T(256)S(1)} %bitcast.36), kind=kCustom, calls=%fused_computation | custom fusion | bytes 4096 | tf_op jit(solution)/shard_map/jit(diagonal)/cond/branch_0_fun/gather | solution.py:62
  28.7 0.0 collective-permute-done
  28.7 0.3 fusion.36
  29.0 0.0 collective-permute-done.4
  29.0 0.2 fusion.31
  29.2 0.0 collective-permute-done.2
  29.2 0.2 fusion.33
  29.5 0.0 collective-permute-done.3
  29.5 0.4 fusion.38
  29.8 0.0 collective-permute-done.1
  29.8 0.4 convolution_add_fusion.2
  30.2 0.7 while.13
  30.2 0.1 dynamic_slice.68
  30.3 0.2 fusion.59
  30.6 0.1 dynamic_slice.68
  30.6 0.2 fusion.59
  30.9 0.0 copy-start
  30.9 4.4 %collective-permute-start.6 = (bf16[64,256]{1,0:T(8,128)(2,1)S(1)}, bf16[64,256]{1,0:T(8,128)(2,1)S(1)}, u32[]{:S(2)}, u32[]{:S(2)}) collective-permute-start(bf16[64,256]{1,0:T(8,128)(2,1)S(1)} %convert_element_type.12), channel_id=1, source_target_pairs={{8,0},{16,8},{24,16},{32,24},{40,32},{48,40},{56,48},{64,56},{72,6... | collective-permute-start | bytes 98312 | tf_op jit(solution)/shard_map/ppermute | solution.py:26
  35.3 1.9 %collective-permute-start.5 = (bf16[64,256]{1,0:T(8,128)(2,1)S(1)}, bf16[64,256]{1,0:T(8,128)(2,1)S(1)}, u32[]{:S(2)}, u32[]{:S(2)}) collective-permute-start(bf16[64,256]{1,0:T(8,128)(2,1)S(1)} %convert_element_type.12), channel_id=1, source_target_pairs={{0,8},{8,16},{16,24},{24,32},{32,40},{40,48},{48,56},{56,64},{64,7... | collective-permute-start | bytes 98312 | tf_op jit(solution)/shard_map/ppermute | solution.py:24
  37.3 0.0 collective-permute-done.6
  37.3 5.4 %collective-permute-done.5 = bf16[64,256]{1,0:T(8,128)(2,1)S(1)} collective-permute-done((bf16[64,256]{1,0:T(8,128)(2,1)S(1)}, bf16[64,256]{1,0:T(8,128)(2,1)S(1)}, u32[]{:S(2)}, u32[]{:S(2)}) %collective-permute-start.5) | collective-permute-done | bytes 32800 | tf_op jit(solution)/shard_map/ppermute | solution.py:24
  42.7 1.0 stack.2
  43.7 0.0 copy-done
  43.7 10.9 %all-to-all-start.1 = ((bf16[8,64,768]{2,1,0:T(8,128)(2,1)}), bf16[8,64,768]{2,1,0:T(8,128)(2,1)S(1)}, u32[]{:S(2)}, u32[]{:S(2)}) async-start(bf16[8,64,768]{2,1,0:T(8,128)(2,1)} %stack.2), calls=%async_computation.1 | async-start | bytes 1572864 | tf_op jit(solution)/shard_map/all_to_all | solution.py:86
  54.6 0.5 all_to_all.17
  55.1 0.8 copy.6
  55.9 20.0 %all-to-all-done.1 = bf16[8,64,768]{2,1,0:T(8,128)(2,1)S(1)} async-done(((bf16[8,64,768]{2,1,0:T(8,128)(2,1)}), bf16[8,64,768]{2,1,0:T(8,128)(2,1)S(1)}, u32[]{:S(2)}, u32[]{:S(2)}) %all-to-all-start.1) | async-done | bytes 786464 | tf_op jit(solution)/shard_map/all_to_all | solution.py:86
  75.8 3.5 %all-to-all-start = ((bf16[64,8,272]{2,0,1:T(8,128)(2,1)}), bf16[64,8,272]{2,0,1:T(8,128)(2,1)S(1)}, u32[]{:S(2)}, u32[]{:S(2)}) async-start(bf16[64,8,272]{2,0,1:T(8,128)(2,1)} %copy.6), calls=%async_computation | async-start | bytes 786432 | tf_op jit(solution)/shard_map/all_to_all | solution.py:97
  79.3 0.3 fusion.18
  79.6 1.0 fusion.12
  80.5 0.3 fusion.14
  80.8 11.8 %all-to-all-done = bf16[64,8,272]{2,0,1:T(8,128)(2,1)S(1)} async-done(((bf16[64,8,272]{2,0,1:T(8,128)(2,1)}), bf16[64,8,272]{2,0,1:T(8,128)(2,1)S(1)}, u32[]{:S(2)}, u32[]{:S(2)}) %all-to-all-start) | async-done | bytes 278560 | tf_op jit(solution)/shard_map/all_to_all | solution.py:97
  92.6 0.3 fusion.20
  92.9 0.0 copy-start.2
  92.9 2.3 %gather_fusion.1 = f32[256]{0:T(256)S(1)} fusion(f32[256,256]{1,0:T(8,128)S(1)} %fusion.18, s32[256]{0:T(256)S(1)} %bitcast.37), kind=kCustom, calls=%fused_computation.1 | custom fusion | bytes 4096 | tf_op jit(solution)/shard_map/jit(diagonal)/cond/branch_0_fun/gather | solution.py:94
  95.2 0.3 fusion.22
  95.6 0.3 convolution_add_fusion.1
  95.9 0.0 copy-done.2
  95.9 1.0 %fusion.11 = bf16[272,256]{1,0:T(8,128)(2,1)} fusion(f32[272,256]{1,0:T(8,128)S(1)} %fusion.20, f32[272,256]{1,0:T(8,128)S(1)} %convolution_add_fusion.1, f32[256,256]{1,0:T(8,128)S(1)} %copy-done.2, s32[]{:T(128)S(6)} %select_n.38, bf16[128,256]{1,0:T(8,128)(2,1)S(1)} %collective-permute-done.4, f32[256]{0:T(256)S(1)} %broadcast_maximum_fusion, ...), kind=kOutput, calls=%fused_computation.18 | convolution fusion | flops 214396928 | bytes 1165312 | tf_op jit(solution)/shard_map/dot_general | solution.py:107
  (11 shorter events, 0.1 us)
Async XLA Ops:
  3.4 26.0 %collective-permute-start.3 = (f32[64,256]{1,0:T(8,128)S(1)}, f32[64,256]{1,0:T(8,128)S(1)}, u32[]{:S(2)}, u32[]{:S(2)}) collective-permute-start(f32[64,256]{1,0:T(8,128)S(1)} %broadcast_select_fusion), channel_id=1, source_target_pairs={{8,0},{16,8},{24,16},{32,24},{40,32},{48,40},{56,48},{64,56},{72,6... | collective-permute-start | bytes 196616 | tf_op jit(solution)/shard_map/ppermute | solution.py:26
  7.3 22.5 %collective-permute-start.1 = (f32[64,256]{1,0:T(8,128)S(1)}, f32[64,256]{1,0:T(8,128)S(1)}, u32[]{:S(2)}, u32[]{:S(2)}) collective-permute-start(f32[64,256]{1,0:T(8,128)S(1)} %broadcast_select_fusion), channel_id=1, source_target_pairs={{0,8},{8,16},{16,24},{24,32},{32,40},{40,48},{48,56},{56,64},{64,7... | collective-permute-start | bytes 196616 | tf_op jit(solution)/shard_map/ppermute | solution.py:24
  10.0 18.7 %collective-permute-start = (bf16[64,128]{1,0:T(8,128)(2,1)S(1)}, bf16[64,128]{1,0:T(8,128)(2,1)S(1)}, u32[]{:S(2)}, u32[]{:S(2)}) collective-permute-start(bf16[64,128]{1,0:T(8,128)(2,1)S(1)} %slice.20), channel_id=1, source_target_pairs={{8,0},{16,8},{24,16},{32,24},{40,32},{48,40},{56,48},{64,56},{72,6... | collective-permute-start | bytes 49160 | tf_op jit(solution)/shard_map/ppermute | solution.py:13
  15.8 10.0 %copy-start.1 = (bf16[64,2048]{1,0:T(8,128)(2,1)S(1)}, bf16[64,2048]{1,0:T(8,128)(2,1)}, u32[]{:S(2)}) copy-start(bf16[64,2048]{1,0:T(8,128)(2,1)} %param.6) | copy-start | bytes 786436
  18.1 11.2 %collective-permute-start.2 = (bf16[128,256]{1,0:T(8,128)(2,1)S(1)}, bf16[128,256]{1,0:T(8,128)(2,1)S(1)}, u32[]{:S(2)}, u32[]{:S(2)}) collective-permute-start(bf16[128,256]{1,0:T(8,128)(2,1)S(1)} %get-tuple-element.124), channel_id=1, source_target_pairs={{0,8},{8,16},{16,24},{24,32},{32,40},{40,48},{48,56},{56,64},{64,7... | collective-permute-start | bytes 196616 | tf_op jit(solution)/shard_map/ppermute | solution.py:13
  20.0 9.0 %collective-permute-start.4 = (bf16[128,256]{1,0:T(8,128)(2,1)S(1)}, bf16[128,256]{1,0:T(8,128)(2,1)S(1)}, u32[]{:S(2)}, u32[]{:S(2)}) collective-permute-start(bf16[128,256]{1,0:T(8,128)(2,1)S(1)} %get-tuple-element.125), channel_id=1, source_target_pairs={{8,0},{16,8},{24,16},{32,24},{40,32},{48,40},{56,48},{64,56},{72,6... | collective-permute-start | bytes 196616 | tf_op jit(solution)/shard_map/ppermute | solution.py:13
  30.9 12.8 %copy-start = (f32[64,256]{1,0:T(8,128)}, f32[64,256]{1,0:T(8,128)S(1)}, u32[]{:S(2)}) copy-start(f32[64,256]{1,0:T(8,128)S(1)} %get-tuple-element.109) | copy-start | bytes 196612
  30.9 6.3 %collective-permute-start.6 = (bf16[64,256]{1,0:T(8,128)(2,1)S(1)}, bf16[64,256]{1,0:T(8,128)(2,1)S(1)}, u32[]{:S(2)}, u32[]{:S(2)}) collective-permute-start(bf16[64,256]{1,0:T(8,128)(2,1)S(1)} %convert_element_type.12), channel_id=1, source_target_pairs={{8,0},{16,8},{24,16},{32,24},{40,32},{48,40},{56,48},{64,56},{72,6... | collective-permute-start | bytes 98312 | tf_op jit(solution)/shard_map/ppermute | solution.py:26
  35.3 7.3 %collective-permute-start.5 = (bf16[64,256]{1,0:T(8,128)(2,1)S(1)}, bf16[64,256]{1,0:T(8,128)(2,1)S(1)}, u32[]{:S(2)}, u32[]{:S(2)}) collective-permute-start(bf16[64,256]{1,0:T(8,128)(2,1)S(1)} %convert_element_type.12), channel_id=1, source_target_pairs={{0,8},{8,16},{16,24},{24,32},{32,40},{40,48},{48,56},{56,64},{64,7... | collective-permute-start | bytes 98312 | tf_op jit(solution)/shard_map/ppermute | solution.py:24
  43.7 32.2 %all-to-all-start.1 = ((bf16[8,64,768]{2,1,0:T(8,128)(2,1)}), bf16[8,64,768]{2,1,0:T(8,128)(2,1)S(1)}, u32[]{:S(2)}, u32[]{:S(2)}) async-start(bf16[8,64,768]{2,1,0:T(8,128)(2,1)} %stack.2), calls=%async_computation.1 | async-start | bytes 1572864 | tf_op jit(solution)/shard_map/all_to_all | solution.py:86
  75.8 16.7 %all-to-all-start = ((bf16[64,8,272]{2,0,1:T(8,128)(2,1)}), bf16[64,8,272]{2,0,1:T(8,128)(2,1)S(1)}, u32[]{:S(2)}, u32[]{:S(2)}) async-start(bf16[64,8,272]{2,0,1:T(8,128)(2,1)} %copy.6), calls=%async_computation | async-start | bytes 786432 | tf_op jit(solution)/shard_map/all_to_all | solution.py:97
  92.9 3.0 %copy-start.2 = (f32[256,256]{1,0:T(8,128)S(1)}, f32[256,256]{1,0:T(8,128)}, u32[]{:S(2)}) copy-start(f32[256,256]{1,0:T(8,128)} %fusion.12) | copy-start | bytes 786436
